TPU v7x, 32 devices: a whole 2x2x4 slice. The times are simulated.
32 devices in a mesh: arc: 8 (over y, x, core), mas: 4 (over z).
Axes of the slice: x: 2, y: 2, z: 4, core: 2. Of those that a mesh axis runs over, the one named last changes fastest.
Arguments:
- jac: bfloat16 [8, 16, 1024, 256], P('arc', 'mas')
- resid: float32 [8, 1024], P('arc'), may hold values from -6 to 6
- counts: int32 [8], P('arc'), may hold values from 512 to 1024
- vis: int32 [8, 16], P('arc'), may hold values from 0 to 39, as said below
- xcur: float32 [40, 256], P('mas'), may hold values from -6 to 6
- damp: float32 [40, 256], P('mas'), may hold values from 2 to 20
Outputs:
- updated: float32 [40, 256], P('mas')
- postfit: float32 [8, 1024], P('arc', 'mas')
Inputs may be any that keep to these rules, and one draw needn't show every extreme that they name: `vis`: each row names 16 distinct blocks; block b is held by index b // 10 of mas.
All inputs are finite; a program needn't handle non-finite values.
Results may differ from a plain program's by a relative error of at most 0.0003.
Values sent between devices are 32-bit elements; how exact they have to be, the bound alone decides.
A program may use at most 64 MiB of HBM per device.

v0:
```python
import jax
import jax.numpy as jnp
from jax import lax
from jax.sharding import PartitionSpec as P

ITERS = 4


def per_device(jac, resid, counts, vis, xcur, damp):
    mas_count = lax.axis_size("mas")
    mas_pos = lax.axis_index("mas")
    block_count = xcur.shape[0]
    slot_count = jac.shape[1]
    row_count = jac.shape[2]
    partials = jac[0]
    listed = vis[0]
    my_blocks = lax.dynamic_slice_in_dim(listed, mas_pos * slot_count, slot_count)
    valid_rows = jnp.arange(row_count) < counts[0]
    prefit = jnp.where(valid_rows, resid[0], 0.0)

    def spread(slot_terms):
        onehot = (my_blocks[:, None] == jnp.arange(block_count * mas_count)[None, :]).astype(
            jnp.float32
        )
        dense_sum = jnp.einsum("vn,vm->nm", onehot, slot_terms, precision=lax.Precision.HIGHEST)
        partial_sum = lax.psum_scatter(dense_sum, "mas", scatter_dimension=0, tiled=True)
        return lax.psum(partial_sum, "arc")

    def fetch(vector):
        gathered = lax.all_gather(vector, "mas", axis=0, tiled=True)
        return jnp.take(gathered, my_blocks, axis=0)

    def forward(slot_values):
        return jnp.einsum("vrm,vm->r", partials, slot_values, precision=lax.Precision.HIGHEST)

    def backward(row_values):
        return jnp.einsum("vrm,r->vm", partials, row_values, precision=lax.Precision.HIGHEST)

    def squares(remain):
        return lax.psum(jnp.sum(remain * remain), "mas")

    rhs = spread(backward(prefit))
    delta = jnp.zeros_like(rhs)
    remain = rhs
    direction = rhs
    norm_now = squares(remain)
    row_share = row_count // mas_count
    for iteration in range(ITERS):
        image_part = forward(fetch(direction))
        image_rows = jnp.where(valid_rows, lax.psum(image_part, "mas"), 0.0)
        applied = spread(backward(image_rows)) + damp * direction
        curvature = lax.psum(jnp.sum(direction * applied), "mas")
        step_len = norm_now / curvature
        delta = delta + step_len * direction
        remain = remain - step_len * applied
        norm_next = squares(remain)
        direction = remain + norm_next / norm_now * direction
        norm_now = norm_next
    change = forward(fetch(delta))
    post_sum = lax.psum_scatter(change[None, :], "mas", scatter_dimension=1, tiled=True)
    prefit_share = lax.dynamic_slice_in_dim(prefit, mas_pos * row_share, row_share)
    valid_share = lax.dynamic_slice_in_dim(valid_rows, mas_pos * row_share, row_share)
    postfit = jnp.where(valid_share, prefit_share - post_sum[0], 0.0)
    return (xcur + delta, postfit[None, :])


def solution(mesh):
    return jax.shard_map(
        per_device,
        mesh=mesh,
        in_specs=(
            P("arc", "mas", None, None),
            P("arc", None),
            P("arc"),
            P("arc", None),
            P("mas", None),
            P("mas", None),
        ),
        out_specs=(P("mas", None), P("arc", "mas")),
        check_vma=False,
    )
```

profile of v0, /device:TPU:0, one launch (start us, length us, event | category | flops | bytes accessed | tf_op | source)
XLA Modules:
  0.0 446.2 jit_solution(12359702845204120861)
XLA Ops:
  10.7 21.2 %all-reduce = f32[40,256]{1,0:T(8,128)S(1)} all-reduce(f32[40,256]{1,0:T(8,128)S(1)} %fusion.33), channel_id=2, replica_groups=mesh['arc'=8,'mas'=4] {'mas'}, use_global_device_ids=true, to_apply=%region_0.1.clone | all-reduce | flops 10240 | bytes 81920
  33.2 22.3 %psum.119 = f32[10,256]{1,0:T(8,128)S(1)} all-reduce(f32[10,256]{1,0:T(8,128)S(1)} %constant_dynamic-slice_fusion.4), channel_id=1, replica_groups=mesh['arc'=8,'mas'=4] {'arc'}, use_global_device_ids=true, to_apply=%region_1.2 | all-reduce | flops 2560 | bytes 20480 | tf_op jit(solution)/shard_map/psum | solution.py:27
  55.5 13.1 %all-gather = f32[4,10,256]{2,1,0:T(8,128)S(1)} all-gather(f32[1,10,256]{2,1,0:T(8,128)S(1)} %bitcast.95), channel_id=1, replica_groups=mesh['arc'=8,'mas'=4] {'mas'}, dimensions={0}, use_global_device_ids=true | all-gather | bytes 51200 | tf_op jit(solution)/shard_map/all_gather | solution.py:30
  69.3 1.7 fusion.16
  71.0 8.5 %psum.121 = f32[1024]{0:T(1024)S(1)} all-reduce(f32[1024]{0:T(1024)S(1)} %bitcast.100), channel_id=1, replica_groups=mesh['arc'=8,'mas'=4] {'mas'}, use_global_device_ids=true, to_apply=%region_4.6 | all-reduce | flops 1024 | bytes 8192 | tf_op jit(solution)/shard_map/psum | solution.py:50
  80.7 17.9 %all-reduce.1 = f32[40,256]{1,0:T(8,128)S(1)} all-reduce(f32[40,256]{1,0:T(8,128)S(1)} %fusion.31), channel_id=3, replica_groups=mesh['arc'=8,'mas'=4] {'mas'}, use_global_device_ids=true, to_apply=%region_5.7.clone | all-reduce | flops 10240 | bytes 81920
  98.7 22.3 %psum.122 = f32[10,256]{1,0:T(8,128)S(1)} all-reduce(f32[10,256]{1,0:T(8,128)S(1)} %constant_dynamic-slice_fusion.3), channel_id=1, replica_groups=mesh['arc'=8,'mas'=4] {'arc'}, use_global_device_ids=true, to_apply=%region_6.8 | all-reduce | flops 2560 | bytes 20480 | tf_op jit(solution)/shard_map/psum | solution.py:27
  121.7 9.1 %all-reduce.5 = (f32[]{:T(128)}, f32[]{:T(128)}) all-reduce(f32[]{:T(128)} %get-tuple-element.4, f32[]{:T(128)} %get-tuple-element.3), channel_id=1, replica_groups=mesh['arc'=8,'mas'=4] {'mas'}, use_global_device_ids=true, to_apply=%region_3.4 | all-reduce | flops 2 | bytes 16 | tf_op jit(solution)/shard_map/psum | solution.py:40
  132.6 10.9 %psum.124 = f32[]{:T(128)} all-reduce(f32[]{:T(128)} %get-tuple-element.13), channel_id=1, replica_groups=mesh['arc'=8,'mas'=4] {'mas'}, use_global_device_ids=true, to_apply=%region_10.12 | all-reduce | flops 1 | bytes 8 | tf_op jit(solution)/shard_map/psum | solution.py:40
  144.8 13.2 %all-gather.1 = f32[4,10,256]{2,1,0:T(8,128)S(1)} all-gather(f32[1,10,256]{2,1,0:T(8,128)S(1)} %fusion.59), channel_id=1, replica_groups=mesh['arc'=8,'mas'=4] {'mas'}, dimensions={0}, use_global_device_ids=true | all-gather | bytes 51200 | tf_op jit(solution)/shard_map/all_gather | solution.py:30
  158.6 1.7 fusion.12
  160.3 8.4 %psum.125 = f32[1024]{0:T(1024)S(1)} all-reduce(f32[1024]{0:T(1024)S(1)} %bitcast.102), channel_id=1, replica_groups=mesh['arc'=8,'mas'=4] {'mas'}, use_global_device_ids=true, to_apply=%region_11.13 | all-reduce | flops 1024 | bytes 8192 | tf_op jit(solution)/shard_map/psum | solution.py:50
  170.0 18.0 %all-reduce.2 = f32[40,256]{1,0:T(8,128)S(1)} all-reduce(f32[40,256]{1,0:T(8,128)S(1)} %fusion.29), channel_id=4, replica_groups=mesh['arc'=8,'mas'=4] {'mas'}, use_global_device_ids=true, to_apply=%region_12.14.clone | all-reduce | flops 10240 | bytes 81920
  188.0 22.3 %psum.126 = f32[10,256]{1,0:T(8,128)S(1)} all-reduce(f32[10,256]{1,0:T(8,128)S(1)} %constant_dynamic-slice_fusion.2), channel_id=1, replica_groups=mesh['arc'=8,'mas'=4] {'arc'}, use_global_device_ids=true, to_apply=%region_13.15 | all-reduce | flops 2560 | bytes 20480 | tf_op jit(solution)/shard_map/psum | solution.py:27
  211.0 9.1 %psum.127 = f32[]{:T(128)} all-reduce(f32[]{:T(128)} %multiply_reduce_fusion.4), channel_id=1, replica_groups=mesh['arc'=8,'mas'=4] {'mas'}, use_global_device_ids=true, to_apply=%region_15.17 | all-reduce | flops 1 | bytes 8 | tf_op jit(solution)/shard_map/psum | solution.py:52
  222.1 11.0 %psum.128 = f32[]{:T(128)} all-reduce(f32[]{:T(128)} %get-tuple-element.11), channel_id=1, replica_groups=mesh['arc'=8,'mas'=4] {'mas'}, use_global_device_ids=true, to_apply=%region_17.19 | all-reduce | flops 1 | bytes 8 | tf_op jit(solution)/shard_map/psum | solution.py:40
  234.3 13.1 %all-gather.2 = f32[4,10,256]{2,1,0:T(8,128)S(1)} all-gather(f32[1,10,256]{2,1,0:T(8,128)S(1)} %bitcast.96), channel_id=1, replica_groups=mesh['arc'=8,'mas'=4] {'mas'}, dimensions={0}, use_global_device_ids=true | all-gather | bytes 51200 | tf_op jit(solution)/shard_map/all_gather | solution.py:30
  248.1 1.7 fusion.8
  249.8 8.4 %psum.129 = f32[1024]{0:T(1024)S(1)} all-reduce(f32[1024]{0:T(1024)S(1)} %bitcast.104), channel_id=1, replica_groups=mesh['arc'=8,'mas'=4] {'mas'}, use_global_device_ids=true, to_apply=%region_18.20 | all-reduce | flops 1024 | bytes 8192 | tf_op jit(solution)/shard_map/psum | solution.py:50
  259.4 18.0 %all-reduce.3 = f32[40,256]{1,0:T(8,128)S(1)} all-reduce(f32[40,256]{1,0:T(8,128)S(1)} %fusion.27), channel_id=5, replica_groups=mesh['arc'=8,'mas'=4] {'mas'}, use_global_device_ids=true, to_apply=%region_19.21.clone | all-reduce | flops 10240 | bytes 81920
  277.5 22.4 %psum.130 = f32[10,256]{1,0:T(8,128)S(1)} all-reduce(f32[10,256]{1,0:T(8,128)S(1)} %constant_dynamic-slice_fusion.1), channel_id=1, replica_groups=mesh['arc'=8,'mas'=4] {'arc'}, use_global_device_ids=true, to_apply=%region_20.22 | all-reduce | flops 2560 | bytes 20480 | tf_op jit(solution)/shard_map/psum | solution.py:27
  300.4 9.0 %psum.131 = f32[]{:T(128)} all-reduce(f32[]{:T(128)} %multiply_reduce_fusion.2), channel_id=1, replica_groups=mesh['arc'=8,'mas'=4] {'mas'}, use_global_device_ids=true, to_apply=%region_22.24 | all-reduce | flops 1 | bytes 8 | tf_op jit(solution)/shard_map/psum | solution.py:52
  311.3 11.0 %psum.132 = f32[]{:T(128)} all-reduce(f32[]{:T(128)} %get-tuple-element.9), channel_id=1, replica_groups=mesh['arc'=8,'mas'=4] {'mas'}, use_global_device_ids=true, to_apply=%region_24.26 | all-reduce | flops 1 | bytes 8 | tf_op jit(solution)/shard_map/psum | solution.py:40
  323.5 13.1 %all-gather.3 = f32[4,10,256]{2,1,0:T(8,128)S(1)} all-gather(f32[1,10,256]{2,1,0:T(8,128)S(1)} %fusion.51), channel_id=1, replica_groups=mesh['arc'=8,'mas'=4] {'mas'}, dimensions={0}, use_global_device_ids=true | all-gather | bytes 51200 | tf_op jit(solution)/shard_map/all_gather | solution.py:30
  337.3 1.7 fusion.4
  339.0 8.4 %psum.133 = f32[1024]{0:T(1024)S(1)} all-reduce(f32[1024]{0:T(1024)S(1)} %bitcast.106), channel_id=1, replica_groups=mesh['arc'=8,'mas'=4] {'mas'}, use_global_device_ids=true, to_apply=%region_25.27 | all-reduce | flops 1024 | bytes 8192 | tf_op jit(solution)/shard_map/psum | solution.py:50
  348.6 18.0 %all-reduce.4 = f32[40,256]{1,0:T(8,128)S(1)} all-reduce(f32[40,256]{1,0:T(8,128)S(1)} %fusion.25), channel_id=6, replica_groups=mesh['arc'=8,'mas'=4] {'mas'}, use_global_device_ids=true, to_apply=%region_26.28.clone | all-reduce | flops 10240 | bytes 81920
  366.7 22.3 %psum.134 = f32[10,256]{1,0:T(8,128)S(1)} all-reduce(f32[10,256]{1,0:T(8,128)S(1)} %constant_dynamic-slice_fusion), channel_id=1, replica_groups=mesh['arc'=8,'mas'=4] {'arc'}, use_global_device_ids=true, to_apply=%region_27.29 | all-reduce | flops 2560 | bytes 20480 | tf_op jit(solution)/shard_map/psum | solution.py:27
  389.7 9.1 %psum.135 = f32[]{:T(128)} all-reduce(f32[]{:T(128)} %multiply_reduce_fusion), channel_id=1, replica_groups=mesh['arc'=8,'mas'=4] {'mas'}, use_global_device_ids=true, to_apply=%region_29.31 | all-reduce | flops 1 | bytes 8 | tf_op jit(solution)/shard_map/psum | solution.py:52
  400.7 13.1 %all-gather.4 = f32[4,10,256]{2,1,0:T(8,128)S(1)} all-gather(f32[1,10,256]{2,1,0:T(8,128)S(1)} %bitcast.98), channel_id=1, replica_groups=mesh['arc'=8,'mas'=4] {'mas'}, dimensions={0}, use_global_device_ids=true | all-gather | bytes 51200 | tf_op jit(solution)/shard_map/all_gather | solution.py:30
  414.5 2.5 fusion.20
  417.1 20.6 %reduce-scatter.4.cloned.1.call-done = f32[256,1]{1,0:T(8,128)} async-done(((f32[1024,1]{1,0:T(8,128)}), f32[256,1]{1,0:T(8,128)}) %reduce-scatter.4.cloned.1.call-update) | async-done | bytes 1040
  (65 shorter events, 18.3 us)
Async XLA Ops:
  7.2 1.6 copy-start
  7.2 24.7 %copy-start.4 = (u32[32]{0:T(128)S(1)}, u32[32]{0:T(128)}, u32[]{:S(2)}) copy-start(u32[32]{0:T(128)} %constant.35) | copy-start | bytes 388
  7.2 430.5 %reduce-scatter.4.cloned.1.call-start = ((), (), s32[]{:S(2)}) async-start(), calls=%async_computation.1 | async-start | bytes 655360
  69.3 51.7 %copy-start.1 = (f32[10,256]{1,0:T(8,128)S(1)}, f32[10,256]{1,0:T(8,128)}, u32[]{:S(2)}) copy-start(f32[10,256]{1,0:T(8,128)} %param.13) | copy-start | bytes 30724
  337.3 62.8 %copy-start.3 = (f32[10,256]{1,0:T(8,128)S(1)}, f32[10,256]{1,0:T(8,128)}, u32[]{:S(2)}) copy-start(f32[10,256]{1,0:T(8,128)} %param.12) | copy-start | bytes 30724
  348.3 68.8 %copy-start.2 = (f32[1,1024]{1,0:T(1,128)S(1)}, f32[1,1024]{1,0:T(1,128)}, u32[]{:S(2)}) copy-start(f32[1,1024]{1,0:T(1,128)} %param.9) | copy-start | bytes 12292
Sparse Core Ops, SparseCore 0:
  417.2 20.4 reduce-scatter.3
where the time goes:
time: 447 us; the launch traced here: 446 us
  blocking collectives  373 us (83%)
  between operations  24.7 us (6%)
  waiting for transfers between devices  20.6 us (5%)
  matrix products  16.1 us (4%)
  other arithmetic  7.02 us (2%)
  local copies, waits for them, and re-layouts  4.5 us (1%)
    psum x5, blocking collectives, spread(): return lax.psum(partial_sum, 'arc')  112 us
    unnamed x5, blocking collectives  93.2 us
    all_gather x5, blocking collectives, fetch(): gathered = lax.all_gather(vector, 'mas', axis=0, tiled=True)  65.7 us
    psum x4, blocking collectives, squares(): return lax.psum(jnp.sum(remain * remain), 'mas')  41.9 us
    psum x4, blocking collectives, per_device(): image_rows = jnp.where(valid_rows, lax.psum(image_part, 'mas'), 0.0)  33.7 us
    psum x3, blocking collectives, per_device(): curvature = lax.psum(jnp.sum(direction * applied), 'mas')  27.1 us
    unnamed x2, waiting for transfers between devices  20.6 us
    dot_general x5, matrix products, forward(): jnp.einsum('vrm,vm->r', partials, slot_values, precision=lax.Precision.HI...  9.41 us
  transfers between devices with their start and end apart: 1, of which 1 were waited for; matrix products, arithmetic and copies ran while one was open for 0% of the time, Pallas kernels for 0%

commit v1 on v0

--- a/solution.py
+++ b/solution.py
@@ -4,6 +4,11 @@
 from jax.sharding import PartitionSpec as P
 
 ITERS = 4
+
+
+def gather_and_add(x, name):
+    parts = lax.all_gather(x, name)
+    return jnp.sum(parts, axis=0)
 
 
 def per_device(jac, resid, counts, vis, xcur, damp):
@@ -24,7 +29,7 @@
         )
         dense_sum = jnp.einsum("vn,vm->nm", onehot, slot_terms, precision=lax.Precision.HIGHEST)
         partial_sum = lax.psum_scatter(dense_sum, "mas", scatter_dimension=0, tiled=True)
-        return lax.psum(partial_sum, "arc")
+        return gather_and_add(partial_sum, "arc")
 
     def fetch(vector):
         gathered = lax.all_gather(vector, "mas", axis=0, tiled=True)

time: 447 us -> 380 us (0.85)
  blocking collectives: 373 us -> 306 us
    psum x5 -> x0, blocking collectives: 112 us -> none  [spread(): return lax.psum(partial_sum, 'arc')]
    all_gather x0 -> x5, blocking collectives: none -> 44.1 us  [gather_and_add(): parts = lax.all_gather(x, name)]
where the time goes in v1:
time: 380 us; the launch traced here: 379 us
  blocking collectives  306 us (81%)
  between operations  24.7 us (6%)
  waiting for transfers between devices  20.3 us (5%)
  matrix products  16.2 us (4%)
  other arithmetic  7.1 us (2%)
  local copies, waits for them, and re-layouts  4.5 us (1%)
    unnamed x5, blocking collectives  92.6 us
    all_gather x5, blocking collectives, fetch(): gathered = lax.all_gather(vector, 'mas', axis=0, tiled=True)  65.9 us
    all_gather x5, blocking collectives, gather_and_add(): parts = lax.all_gather(x, name)  44.1 us
    psum x4, blocking collectives, squares(): return lax.psum(jnp.sum(remain * remain), 'mas')  41.5 us
    psum x4, blocking collectives, per_device(): image_rows = jnp.where(valid_rows, lax.psum(image_part, 'mas'), 0.0)  34.3 us
    psum x3, blocking collectives, per_device(): curvature = lax.psum(jnp.sum(direction * applied), 'mas')  27.6 us
    unnamed x2, waiting for transfers between devices  20.3 us
    dot_general x5, matrix products, forward(): jnp.einsum('vrm,vm->r', partials, slot_values, precision=lax.Precision.HI...  9.41 us
  transfers between devices with their start and end apart: 1, of which 1 were waited for; matrix products, arithmetic and copies ran while one was open for 0% of the time, Pallas kernels for 0%

profile of v1, /device:TPU:0, one launch (start us, length us, event | category | flops | bytes accessed | tf_op | source)
XLA Modules:
  0.0 378.8 jit_solution(11289251422591067651)
XLA Ops:
  10.7 21.2 %all-reduce = f32[40,256]{1,0:T(8,128)S(1)} all-reduce(f32[40,256]{1,0:T(8,128)S(1)} %fusion.33), channel_id=7, replica_groups=mesh['arc'=8,'mas'=4] {'mas'}, use_global_device_ids=true, to_apply=%region_0.1.clone | all-reduce | flops 10240 | bytes 81920
  33.2 9.2 %all-gather.5 = f32[8,10,256]{2,1,0:T(8,128)S(1)} all-gather(f32[1,10,256]{2,1,0:T(8,128)S(1)} %dynamic-slice_bitcast_fusion.4), channel_id=2, replica_groups=mesh['arc'=8,'mas'=4] {'arc'}, dimensions={0}, use_global_device_ids=true | all-gather | bytes 92160 | tf_op jit(solution)/shard_map/all_gather | solution.py:10
  42.4 13.1 %all-gather.6 = f32[4,10,256]{2,1,0:T(8,128)S(1)} all-gather(f32[1,10,256]{2,1,0:T(8,128)S(1)} %bitcast.105), channel_id=1, replica_groups=mesh['arc'=8,'mas'=4] {'mas'}, dimensions={0}, use_global_device_ids=true | all-gather | bytes 51200 | tf_op jit(solution)/shard_map/all_gather | solution.py:35
  56.2 1.7 fusion.16
  57.9 8.4 %psum.85 = f32[1024]{0:T(1024)S(1)} all-reduce(f32[1024]{0:T(1024)S(1)} %bitcast.110), channel_id=1, replica_groups=mesh['arc'=8,'mas'=4] {'mas'}, use_global_device_ids=true, to_apply=%region_4.6 | all-reduce | flops 1024 | bytes 8192 | tf_op jit(solution)/shard_map/psum | solution.py:55
  67.6 18.0 %all-reduce.1 = f32[40,256]{1,0:T(8,128)S(1)} all-reduce(f32[40,256]{1,0:T(8,128)S(1)} %fusion.31), channel_id=8, replica_groups=mesh['arc'=8,'mas'=4] {'mas'}, use_global_device_ids=true, to_apply=%region_5.7.clone | all-reduce | flops 10240 | bytes 81920
  85.6 9.2 %all-gather.7 = f32[8,10,256]{2,1,0:T(8,128)S(1)} all-gather(f32[1,10,256]{2,1,0:T(8,128)S(1)} %dynamic-slice_bitcast_fusion.3), channel_id=3, replica_groups=mesh['arc'=8,'mas'=4] {'arc'}, dimensions={0}, use_global_device_ids=true | all-gather | bytes 92160 | tf_op jit(solution)/shard_map/all_gather | solution.py:10
  95.5 9.0 %all-reduce.5 = (f32[]{:T(128)}, f32[]{:T(128)}) all-reduce(f32[]{:T(128)} %get-tuple-element.4, f32[]{:T(128)} %get-tuple-element.3), channel_id=1, replica_groups=mesh['arc'=8,'mas'=4] {'mas'}, use_global_device_ids=true, to_apply=%region_3.4 | all-reduce | flops 2 | bytes 16 | tf_op jit(solution)/shard_map/psum | solution.py:45
  106.3 11.0 %psum.87 = f32[]{:T(128)} all-reduce(f32[]{:T(128)} %get-tuple-element.13), channel_id=1, replica_groups=mesh['arc'=8,'mas'=4] {'mas'}, use_global_device_ids=true, to_apply=%region_10.12 | all-reduce | flops 1 | bytes 8 | tf_op jit(solution)/shard_map/psum | solution.py:45
  118.6 13.1 %all-gather.8 = f32[4,10,256]{2,1,0:T(8,128)S(1)} all-gather(f32[1,10,256]{2,1,0:T(8,128)S(1)} %fusion.59), channel_id=1, replica_groups=mesh['arc'=8,'mas'=4] {'mas'}, dimensions={0}, use_global_device_ids=true | all-gather | bytes 51200 | tf_op jit(solution)/shard_map/all_gather | solution.py:35
  132.4 1.7 fusion.12
  134.1 8.5 %psum.88 = f32[1024]{0:T(1024)S(1)} all-reduce(f32[1024]{0:T(1024)S(1)} %bitcast.112), channel_id=1, replica_groups=mesh['arc'=8,'mas'=4] {'mas'}, use_global_device_ids=true, to_apply=%region_11.13 | all-reduce | flops 1024 | bytes 8192 | tf_op jit(solution)/shard_map/psum | solution.py:55
  143.8 17.9 %all-reduce.2 = f32[40,256]{1,0:T(8,128)S(1)} all-reduce(f32[40,256]{1,0:T(8,128)S(1)} %fusion.29), channel_id=9, replica_groups=mesh['arc'=8,'mas'=4] {'mas'}, use_global_device_ids=true, to_apply=%region_12.14.clone | all-reduce | flops 10240 | bytes 81920
  161.7 8.3 %all-gather.9 = f32[8,10,256]{2,1,0:T(8,128)S(1)} all-gather(f32[1,10,256]{2,1,0:T(8,128)S(1)} %dynamic-slice_bitcast_fusion.2), channel_id=4, replica_groups=mesh['arc'=8,'mas'=4] {'arc'}, dimensions={0}, use_global_device_ids=true | all-gather | bytes 92160 | tf_op jit(solution)/shard_map/all_gather | solution.py:10
  170.7 9.2 %psum.89 = f32[]{:T(128)} all-reduce(f32[]{:T(128)} %multiply_reduce_fusion.4), channel_id=1, replica_groups=mesh['arc'=8,'mas'=4] {'mas'}, use_global_device_ids=true, to_apply=%region_15.17 | all-reduce | flops 1 | bytes 8 | tf_op jit(solution)/shard_map/psum | solution.py:57
  181.9 10.9 %psum.90 = f32[]{:T(128)} all-reduce(f32[]{:T(128)} %get-tuple-element.11), channel_id=1, replica_groups=mesh['arc'=8,'mas'=4] {'mas'}, use_global_device_ids=true, to_apply=%region_17.19 | all-reduce | flops 1 | bytes 8 | tf_op jit(solution)/shard_map/psum | solution.py:45
  194.0 13.1 %all-gather.10 = f32[4,10,256]{2,1,0:T(8,128)S(1)} all-gather(f32[1,10,256]{2,1,0:T(8,128)S(1)} %bitcast.106), channel_id=1, replica_groups=mesh['arc'=8,'mas'=4] {'mas'}, dimensions={0}, use_global_device_ids=true | all-gather | bytes 51200 | tf_op jit(solution)/shard_map/all_gather | solution.py:35
  207.8 1.7 fusion.8
  209.6 8.7 %psum.91 = f32[1024]{0:T(1024)S(1)} all-reduce(f32[1024]{0:T(1024)S(1)} %bitcast.114), channel_id=1, replica_groups=mesh['arc'=8,'mas'=4] {'mas'}, use_global_device_ids=true, to_apply=%region_18.20 | all-reduce | flops 1024 | bytes 8192 | tf_op jit(solution)/shard_map/psum | solution.py:55
  219.5 17.7 %all-reduce.3 = f32[40,256]{1,0:T(8,128)S(1)} all-reduce(f32[40,256]{1,0:T(8,128)S(1)} %fusion.27), channel_id=10, replica_groups=mesh['arc'=8,'mas'=4] {'mas'}, use_global_device_ids=true, to_apply=%region_19.21.clone | all-reduce | flops 10240 | bytes 81920
  237.2 9.2 %all-gather.11 = f32[8,10,256]{2,1,0:T(8,128)S(1)} all-gather(f32[1,10,256]{2,1,0:T(8,128)S(1)} %dynamic-slice_bitcast_fusion.1), channel_id=5, replica_groups=mesh['arc'=8,'mas'=4] {'arc'}, dimensions={0}, use_global_device_ids=true | all-gather | bytes 92160 | tf_op jit(solution)/shard_map/all_gather | solution.py:10
  247.0 9.2 %psum.92 = f32[]{:T(128)} all-reduce(f32[]{:T(128)} %multiply_reduce_fusion.2), channel_id=1, replica_groups=mesh['arc'=8,'mas'=4] {'mas'}, use_global_device_ids=true, to_apply=%region_22.24 | all-reduce | flops 1 | bytes 8 | tf_op jit(solution)/shard_map/psum | solution.py:57
  258.1 10.7 %psum.93 = f32[]{:T(128)} all-reduce(f32[]{:T(128)} %get-tuple-element.9), channel_id=1, replica_groups=mesh['arc'=8,'mas'=4] {'mas'}, use_global_device_ids=true, to_apply=%region_24.26 | all-reduce | flops 1 | bytes 8 | tf_op jit(solution)/shard_map/psum | solution.py:45
  270.1 13.3 %all-gather.12 = f32[4,10,256]{2,1,0:T(8,128)S(1)} all-gather(f32[1,10,256]{2,1,0:T(8,128)S(1)} %fusion.51), channel_id=1, replica_groups=mesh['arc'=8,'mas'=4] {'mas'}, dimensions={0}, use_global_device_ids=true | all-gather | bytes 51200 | tf_op jit(solution)/shard_map/all_gather | solution.py:35
  284.1 1.7 fusion.4
  285.8 8.6 %psum.94 = f32[1024]{0:T(1024)S(1)} all-reduce(f32[1024]{0:T(1024)S(1)} %bitcast.116), channel_id=1, replica_groups=mesh['arc'=8,'mas'=4] {'mas'}, use_global_device_ids=true, to_apply=%region_25.27 | all-reduce | flops 1024 | bytes 8192 | tf_op jit(solution)/shard_map/psum | solution.py:55
  295.6 17.8 %all-reduce.4 = f32[40,256]{1,0:T(8,128)S(1)} all-reduce(f32[40,256]{1,0:T(8,128)S(1)} %fusion.25), channel_id=11, replica_groups=mesh['arc'=8,'mas'=4] {'mas'}, use_global_device_ids=true, to_apply=%region_26.28.clone | all-reduce | flops 10240 | bytes 81920
  313.5 8.3 %all-gather.13 = f32[8,10,256]{2,1,0:T(8,128)S(1)} all-gather(f32[1,10,256]{2,1,0:T(8,128)S(1)} %dynamic-slice_bitcast_fusion), channel_id=6, replica_groups=mesh['arc'=8,'mas'=4] {'arc'}, dimensions={0}, use_global_device_ids=true | all-gather | bytes 92160 | tf_op jit(solution)/shard_map/all_gather | solution.py:10
  322.4 9.2 %psum.95 = f32[]{:T(128)} all-reduce(f32[]{:T(128)} %multiply_reduce_fusion), channel_id=1, replica_groups=mesh['arc'=8,'mas'=4] {'mas'}, use_global_device_ids=true, to_apply=%region_29.31 | all-reduce | flops 1 | bytes 8 | tf_op jit(solution)/shard_map/psum | solution.py:57
  333.6 13.2 %all-gather.14 = f32[4,10,256]{2,1,0:T(8,128)S(1)} all-gather(f32[1,10,256]{2,1,0:T(8,128)S(1)} %bitcast.108), channel_id=1, replica_groups=mesh['arc'=8,'mas'=4] {'mas'}, dimensions={0}, use_global_device_ids=true | all-gather | bytes 51200 | tf_op jit(solution)/shard_map/all_gather | solution.py:35
  347.5 2.6 fusion.20
  350.1 20.3 %reduce-scatter.4.cloned.1.call-done = f32[256,1]{1,0:T(8,128)} async-done(((f32[1024,1]{1,0:T(8,128)}), f32[256,1]{1,0:T(8,128)}) %reduce-scatter.4.cloned.1.call-update) | async-done | bytes 1040
  (70 shorter events, 18.4 us)
Async XLA Ops:
  7.2 1.6 copy-start
  7.2 24.7 %copy-start.4 = (u32[32]{0:T(128)S(1)}, u32[32]{0:T(128)}, u32[]{:S(2)}) copy-start(u32[32]{0:T(128)} %constant.35) | copy-start | bytes 388
  7.2 363.2 %reduce-scatter.4.cloned.1.call-start = ((), (), s32[]{:S(2)}) async-start(), calls=%async_computation.1 | async-start | bytes 655360
  56.2 38.6 %copy-start.1 = (f32[10,256]{1,0:T(8,128)S(1)}, f32[10,256]{1,0:T(8,128)}, u32[]{:S(2)}) copy-start(f32[10,256]{1,0:T(8,128)} %param.13) | copy-start | bytes 30724
  284.1 48.9 %copy-start.3 = (f32[10,256]{1,0:T(8,128)S(1)}, f32[10,256]{1,0:T(8,128)}, u32[]{:S(2)}) copy-start(f32[10,256]{1,0:T(8,128)} %param.12) | copy-start | bytes 30724
  295.3 54.7 %copy-start.2 = (f32[1,1024]{1,0:T(1,128)S(1)}, f32[1,1024]{1,0:T(1,128)}, u32[]{:S(2)}) copy-start(f32[1,1024]{1,0:T(1,128)} %param.9) | copy-start | bytes 12292
Sparse Core Ops, SparseCore 0:
  350.2 20.1 reduce-scatter.3
